TPU v7x, 256 devices: a whole 4x4x8 slice. The times are simulated.
256 devices in a mesh: wide: 64 (over z, y, core), narrow: 4 (over x).
Axes of the slice: x: 4, y: 4, z: 8, core: 2. Of those that a mesh axis runs over, the one named last changes fastest.
Arguments:
- panel: float32 [131072, 128], P(('wide', 'narrow')), may hold values from -40 to 40
- trailing: float32 [131072, 256], P(('wide', 'narrow')), may hold values from -40 to 40
Outputs:
- q_factor: float32 [131072, 128], P(('wide', 'narrow'))
- r_factor: float32 [128, 128], replicated
- projection: float32 [128, 256], replicated
- updated: float32 [131072, 256], P(('wide', 'narrow'))
All inputs are finite; a program needn't handle non-finite values.
Results may differ from a plain program's by a relative error of at most 0.00045.
Values sent between devices are 32-bit elements; how exact they have to be, the bound alone decides.
A program may use at most 64 MiB of HBM per device.

v0:
```python
import jax
import jax.numpy as jnp
from jax import lax
from jax.sharding import PartitionSpec as P


def upper_factor(gram_matrix):
    order = gram_matrix.shape[0]
    columns = jnp.arange(order, dtype=jnp.int32)

    def column_step(index, state):
        work, factor = state
        where = jnp.asarray(index).astype(jnp.int32)
        pivot_row = lax.dynamic_index_in_dim(work, where, 0, keepdims=False)
        pivot = lax.dynamic_index_in_dim(pivot_row, where, 0, keepdims=False)
        new_row = jnp.where(
            columns >= where, pivot_row / jnp.sqrt(pivot), jnp.zeros_like(pivot_row)
        )
        work = work - new_row[:, None] * new_row[None, :]
        factor = lax.dynamic_update_slice_in_dim(factor, new_row[None, :], where, 0)
        return (work, factor)

    start = (gram_matrix, jnp.zeros_like(gram_matrix))
    return lax.fori_loop(0, order, column_step, start)[1]


def inverse_upper(upper_part):
    order = upper_part.shape[0]
    identity = jnp.eye(order, dtype=upper_part.dtype)

    def row_step(count, inverse):
        where = (order - 1 - jnp.asarray(count)).astype(jnp.int32)
        upper_row = lax.dynamic_index_in_dim(upper_part, where, 0, keepdims=False)
        unit_row = lax.dynamic_index_in_dim(identity, where, 0, keepdims=False)
        pivot = lax.dynamic_index_in_dim(upper_row, where, 0, keepdims=False)
        partial_value = jnp.dot(upper_row, inverse, precision=lax.Precision.HIGHEST)
        new_row = (unit_row - partial_value) / pivot
        return lax.dynamic_update_slice_in_dim(inverse, new_row[None, :], where, 0)

    return lax.fori_loop(0, order, row_step, jnp.zeros_like(upper_part))


def product(left, right):
    return jnp.dot(left, right, precision=lax.Precision.HIGHEST, preferred_element_type=jnp.float32)


def on_device(panel, trailing):
    row_total = float(panel.shape[0] * lax.axis_size("wide") * lax.axis_size("narrow"))
    gram_local = product(panel.T, panel) / row_total
    cross_local = product(panel.T, trailing) / row_total
    gram_first, cross_terms = lax.psum((gram_local, cross_local), ("wide", "narrow"))
    first_factor = upper_factor(gram_first)
    basis_rows = product(panel, inverse_upper(first_factor))
    gram_second = lax.psum(product(basis_rows.T, basis_rows) / row_total, ("wide", "narrow"))
    second_factor = upper_factor(gram_second)
    q_factor = product(basis_rows, inverse_upper(second_factor))
    r_factor = product(second_factor, first_factor)
    projection = product(inverse_upper(r_factor).T, cross_terms)
    updated = trailing - product(q_factor, projection)
    return (q_factor, r_factor, projection, updated)


def solution(mesh):
    in_specs = (P(("wide", "narrow"), None), P(("wide", "narrow"), None))
    out_specs = (P(("wide", "narrow"), None), P(), P(), P(("wide", "narrow"), None))
    return jax.shard_map(
        on_device, mesh=mesh, in_specs=in_specs, out_specs=out_specs, check_vma=False
    )
```

profile of v0, /device:TPU:1, one launch (start us, length us, event | category | flops | bytes accessed | tf_op | source)
XLA Modules:
  0.0 1444.5 jit_solution(6588937808590446458)
XLA Ops:
  7.2 0.9 copy-done
  8.1 1.2 convolution_multiply_fusion.2
  9.4 1.3 convolution_multiply_fusion
  10.7 245.3 %all-reduce.4.cloned.1.call-done = f32[128,128]{1,0:T(8,128)} async-done(((f32[128,128]{1,0:T(8,128)}), f32[128,128]{1,0:T(8,128)}) %all-reduce.4.cloned.1.call-update) | async-done | bytes 65552 | tf_op jit(solution)/shard_map/psum | solution.py:51
  256.0 0.8 copy-done.3
  256.8 188.3 %while.89 = (s32[]{:T(128)}, f32[128,128]{1,0:T(8,128)S(1)}, f32[128,128]{1,0:T(8,128)S(1)}, s32[]{:T(128)}, s32[]{:T(128)}, /*index=5*/s32[]{:T(128)}) while((s32[]{:T(128)}, f32[128,128]{1,0:T(8,128)S(1)}, f32[128,128]{1,0:T(8,128)S(1)}, s32[]{:T(128)}, s32[]{:T(128)}, /*index=5*/s32[]{:T(128)}) %tuple.212), condition=%wide.region_2.3_spmd.clone, body=%wide.region_1.0_spmd.clone.sunk | while | flops 33667 | bytes 138357 | solution.py:24
  445.1 185.2 %while.86 = (s32[]{:T(128)}, f32[128,128]{1,0:T(8,128)S(1)}, f32[128,128]{1,0:T(8,128)S(1)}, f32[128,128]{1,0:T(8,128)S(1)}, s32[]{:T(128)}, /*index=5*/s32[]{:T(128)}, s32[]{:T(128)}, s32[]{:T(128)}) while((s32[]{:T(128)}, f32[128,128]{1,0:T(8,128)S(1)}, f32[128,128]{1,0:T(8,128)S(1)}, f32[128,128]{1,0:T(8,128)S(1)}, s32[]{:T(128)}, ...), condition=%wide.region_4.5_spmd, body=%wide.region_3.4_spmd.sunk | while | flops 196871 | bytes 69287 | solution.py:40
  454.4 0.8 fusion.61
  455.9 0.8 fusion.61
  457.3 0.8 fusion.61
  458.8 0.8 fusion.61
  467.5 0.8 fusion.61
  468.9 0.8 fusion.61
  470.3 0.8 fusion.61
  471.8 0.8 fusion.61
  481.9 0.8 fusion.61
  483.4 0.8 fusion.61
  484.8 0.8 fusion.61
  486.3 0.8 fusion.61
  494.9 0.8 fusion.61
  496.4 0.8 fusion.61
  497.8 0.8 fusion.61
  499.3 0.8 fusion.61
  509.4 0.8 fusion.61
  510.9 0.8 fusion.61
  512.3 0.8 fusion.61
  513.8 0.8 fusion.61
  522.4 0.8 fusion.61
  523.9 0.8 fusion.61
  525.3 0.8 fusion.61
  526.8 0.8 fusion.61
  536.9 0.8 fusion.61
  538.3 0.8 fusion.61
  539.8 0.8 fusion.61
  541.2 0.8 fusion.61
  549.9 0.8 fusion.61
  551.4 0.8 fusion.61
  552.8 0.8 fusion.61
  554.3 0.8 fusion.61
  564.4 0.8 fusion.61
  565.8 0.8 fusion.61
  567.3 0.8 fusion.61
  568.7 0.8 fusion.61
  577.4 0.8 fusion.61
  578.9 0.8 fusion.61
  580.3 0.8 fusion.61
  581.8 0.8 fusion.61
  591.9 0.8 fusion.61
  593.3 0.8 fusion.61
  594.8 0.8 fusion.61
  596.2 0.8 fusion.61
  604.9 0.8 fusion.61
  606.3 0.8 fusion.61
  607.8 0.8 fusion.61
  609.2 0.8 fusion.61
  619.4 0.8 fusion.61
  620.8 0.8 fusion.61
  630.8 1.0 convolution_multiply_fusion.1
  631.8 242.9 %all-reduce.6.cloned.1.call-done = (f32[128,128]{1,0:T(8,128)}, f32[128,256]{1,0:T(8,128)}) async-done(((f32[128,128]{1,0:T(8,128)}, f32[128,256]{1,0:T(8,128)}), (f32[128,128]{1,0:T(8,128)}, f32[128,256]{1,0:T(8,128)})) %all-reduce.6.cloned.1.call-update) | async-done | bytes 196624 | tf_op jit(solution)/shard_map/psum | solution.py:54
  874.7 0.8 copy-done.2
  875.5 188.3 %while.90 = (s32[]{:T(128)}, f32[128,128]{1,0:T(8,128)S(1)}, f32[128,128]{1,0:T(8,128)S(1)}, s32[]{:T(128)}, s32[]{:T(128)}, /*index=5*/s32[]{:T(128)}) while((s32[]{:T(128)}, f32[128,128]{1,0:T(8,128)S(1)}, f32[128,128]{1,0:T(8,128)S(1)}, s32[]{:T(128)}, s32[]{:T(128)}, /*index=5*/s32[]{:T(128)}) %tuple.211), condition=%wide.region_7.8_spmd.clone, body=%wide.region_6.7_spmd.clone.sunk | while | flops 33667 | bytes 138357 | solution.py:24
  1064.0 185.2 %while.88 = (s32[]{:T(128)}, f32[128,128]{1,0:T(8,128)S(1)}, f32[128,128]{1,0:T(8,128)S(1)}, f32[128,128]{1,0:T(8,128)S(1)}, s32[]{:T(128)}, /*index=5*/s32[]{:T(128)}, s32[]{:T(128)}, s32[]{:T(128)}) while((s32[]{:T(128)}, f32[128,128]{1,0:T(8,128)S(1)}, f32[128,128]{1,0:T(8,128)S(1)}, f32[128,128]{1,0:T(8,128)S(1)}, s32[]{:T(128)}, ...), condition=%wide.region_11.12_spmd, body=%wide.region_10.11_spmd.sunk | while | flops 196871 | bytes 69287 | solution.py:40
  1249.9 185.2 %while.87 = (s32[]{:T(128)}, f32[128,128]{1,0:T(8,128)S(1)}, f32[128,128]{1,0:T(8,128)S(1)}, f32[128,128]{1,0:T(8,128)S(1)}, s32[]{:T(128)}, /*index=5*/s32[]{:T(128)}, s32[]{:T(128)}, s32[]{:T(128)}) while((s32[]{:T(128)}, f32[128,128]{1,0:T(8,128)S(1)}, f32[128,128]{1,0:T(8,128)S(1)}, f32[128,128]{1,0:T(8,128)S(1)}, s32[]{:T(128)}, ...), condition=%wide.region_9.10_spmd, body=%wide.region_8.9_spmd.sunk | while | flops 196871 | bytes 69287 | solution.py:40
  1436.3 1.4 convolution_subtract_fusion
  (2665 shorter events, 693.3 us)
Async XLA Ops:
  7.2 1.0 copy-start
  7.2 2.2 copy-start.1
  7.2 248.8 %all-reduce.4.cloned.1.call-start = ((), (), s32[]{:S(2)}) async-start(), calls=%async_computation | async-start | bytes 131072 | tf_op jit(solution)/shard_map/psum | solution.py:51
  9.4 865.3 %all-reduce.6.cloned.1.call-start = ((), (), s32[]{:S(2)}) async-start(), calls=%async_computation.1 | async-start | bytes 393216 | tf_op jit(solution)/shard_map/psum | solution.py:54
  256.0 0.8 copy-start.3
  874.7 0.8 copy-start.2
  1249.2 0.6 copy-start.7
  1435.0 0.9 copy-start.6
  1435.6 2.0 copy-start.4
  1436.3 1.4 copy-start.5
Sparse Core Ops, SparseCore 0:
  14.1 241.8 all-reduce.3
  631.9 242.7 all-reduce.5
where the time goes:
time: 1450 us; the launch traced here: 1440 us
  waiting for transfers between devices  488 us (34%)
  local copies, waits for them, and re-layouts  401 us (28%)
  matrix products  313 us (22%)
  loops' own time  202 us (14%)
  other arithmetic  26.6 us (2%)
    dot_general x384, matrix products, row_step(): partial_value = jnp.dot(upper_row, inverse, precision=lax.Precision.HIGHEST)  306 us
    psum x1, waiting for transfers between devices, on_device(): lax.psum((gram_local, cross_local), ('wide', 'narrow'))  245 us
    psum x1, waiting for transfers between devices, on_device(): lax.psum(product(basis_rows.T, basis_rows) / row_total, ('wide', 'narrow'))  243 us
    dynamic_slice x384, local copies, waits for them, and re-layouts, row_step(): pivot = lax.dynamic_index_in_dim(upper_row, where, 0, keepdims=False)  226 us
    another operation x2, loops' own time, upper_factor(): return lax.fori_loop(0, order, column_step, start)[1]  190 us
    dynamic_slice x256, local copies, waits for them, and re-layouts, column_step(): pivot = lax.dynamic_index_in_dim(pivot_row, where, 0, keepdims=False)  151 us
  transfers between devices with their start and end apart: 2, of which 2 were waited for; matrix products, arithmetic and copies ran while one was open for 0% of the time, Pallas kernels for 0%

commit v1 on v0

v1 whole, which is shorter than its diff:
```python
import functools

import jax
import jax.numpy as jnp
from jax import lax
from jax.experimental import pallas as pl
from jax.experimental.pallas import tpu as pltpu
from jax.sharding import PartitionSpec as P

f32 = jnp.float32
bf16 = jnp.bfloat16
HIGHEST = lax.Precision.HIGHEST
MESH = pl.DeviceIdType.MESH

ORDER = 128
TRAIL = 256
NX, NY, NC = 4, 4, 2
SHARES = NX * NY * NC
TILE = 8
WIDTH = 32


def contract(left, right, dims, precision=HIGHEST):
    return lax.dot_general(
        left, right, (dims, ((), ())), precision=precision, preferred_element_type=f32
    )


def two_sum(a, b):
    total = a + b
    part = total - a
    return total, (a - (total - part)) + (b - part)


def slices(values):
    top = jnp.max(jnp.abs(values), axis=0, keepdims=True)
    unit = (top + top * (2.0**-23)) - top
    shift = unit * (1.5 * 2.0**40)
    parts = []
    rest = values
    for _ in range(3):
        part = (rest + shift) - shift
        rest = rest - part
        shift = shift * (2.0**-8)
        parts.append(part.astype(bf16))
    parts.append(rest.astype(bf16))
    return parts


def gram_parts(parts):
    first = contract(parts[0], jnp.concatenate(parts, axis=1), ((0,), (0,)), None)
    second = contract(parts[1], jnp.concatenate(parts[1:], axis=1), ((0,), (0,)), None)
    third = contract(parts[2], parts[2], ((0,), (0,)), None)
    n = ORDER
    cross = first[:, n : 2 * n]
    tail = (first[:, 2 * n : 3 * n] + second[:, n : 2 * n]) + (
        first[:, 3 * n :] + second[:, 2 * n :]
    )
    return first[:, :n], cross + cross.T, (tail + tail.T) + (second[:, :n] + third)


def factor(work):
    order, width = work.shape[0], WIDTH
    rows = lax.broadcasted_iota(jnp.int32, (order, order), 0)
    cols = lax.broadcasted_iota(jnp.int32, (order, order), 1)
    inverse = jnp.where(rows == cols, 1.0, 0.0).astype(f32)
    sub = lax.broadcasted_iota(jnp.int32, (width, order), 0)
    lane = lax.broadcasted_iota(jnp.int32, (width, order), 1)
    uppers, inverses = [], []
    for start in range(0, order, width):
        top, top_inverse = work[:width], inverse[:width]
        column = jnp.stack(
            [
                jnp.broadcast_to(top[:, start + k : start + k + 1], (width, order))
                for k in range(width)
            ]
        )
        pivots = jnp.ones((width, order), f32)
        for i in range(width):
            pivot = column[0, i : i + 1, :]
            pivots = jnp.where(sub == i, pivot, pivots)
            if i + 1 < width:
                ratio = jnp.where(sub > i, column[0] * (1.0 / pivot), 0.0)
                column = column[1:] - ratio[None] * column[1:, i : i + 1, :]
                top = top - ratio * top[i : i + 1, :]
                top_inverse = top_inverse - ratio * top_inverse[i : i + 1, :]
        scale = lax.rsqrt(pivots)
        upper = jnp.where(sub + start <= lane, top * scale, 0.0)
        lower = top_inverse * scale
        uppers.append(upper)
        inverses.append(lower)
        if start + width < order:
            both = jnp.concatenate([upper, lower], axis=1)
            step = contract(upper, both, ((0,), (0,)))[start + width :]
            work = work[width:] - step[:, :order]
            inverse = inverse[width:] - step[:, order:]
    return jnp.concatenate(uppers, axis=0), jnp.concatenate(inverses, axis=0)


def swap(tiles):
    return pltpu.roll(tiles, 4, tiles.ndim - 2)


def halves(left, right):
    left = left.reshape(ORDER // TILE, TILE, ORDER)
    right = swap(right.reshape(ORDER // TILE, TILE, ORDER))
    low = lax.broadcasted_iota(jnp.int32, left.shape, 1) < 4
    return jnp.where(low, left, right), jnp.where(low, right, left)


def unhalve(even, odd):
    low = lax.broadcasted_iota(jnp.int32, even.shape, 1) < 4
    left = jnp.where(low, even, odd)
    right = swap(jnp.where(low, odd, even))
    return left.reshape(ORDER, ORDER), right.reshape(ORDER, ORDER)


def add_up(terms, core):
    sub = lax.broadcasted_iota(jnp.int32, (TILE, ORDER), 0)
    mine = (sub // 4) == core
    total, error = terms[0][:TILE], jnp.zeros((TILE, ORDER), f32)
    plain = [t[TILE:] for t in terms]
    for term in terms[1:]:
        total, more = two_sum(total, term[:TILE])
        error = error + more
    low = error + swap(total + error)
    high = total + low
    rest = low - (high - total)
    while len(plain) > 1:
        plain = [a + b for a, b in zip(plain[::2], plain[1::2])] + (
            [plain[-1]] if len(plain) % 2 else []
        )
    return jnp.where(mine, high, swap(rest)), plain[0]


def reduce_kernel(
    nz, row_total,
    panel_ref, trail_ref, high_ref, low_ref, cross_ref,
    panel, trail, send, rs_in, z_out, z_in, gathered,
    load_sem, rs_send, rs_recv, z_send, z_recv, ag_send, ag_recv,
):
    load_panel = pltpu.make_async_copy(panel_ref, panel, load_sem.at[0])
    load_trail = pltpu.make_async_copy(trail_ref, trail, load_sem.at[1])
    load_panel.start()
    load_trail.start()

    wide, x = lax.axis_index("wide"), lax.axis_index("narrow")
    z, y, core = wide // (NY * NC), (wide // NC) % NY, wide % NC
    share = (x * NY + y) * NC + core

    near = []
    for dx in range(NX):
        for dy in range(NY):
            for dc in range(NC):
                if dx or dy or dc:
                    hops = min(dx, NX - dx) + min(dy, NY - dy)
                    near.append((-hops, dx, dy, dc))
    near = sorted(near)

    def neighbour(dx, dy, dc):
        px, py, pc = (x + dx) % NX, (y + dy) % NY, (core + dc) % NC
        return (px * NY + py) * NC + pc, ((z * NY + py) * NC + pc, px)

    around = [neighbour(dx, dy, dc) for _, dx, dy, dc in near]
    steps = sorted(range(1, nz), key=lambda d: -min(d, nz - d))
    along = [((((z + d) % nz) * NY + y) * NC + core, x) for d in steps]

    barrier = pltpu.get_barrier_semaphore()
    for device in along + [device for _, device in around]:
        pl.semaphore_signal(barrier, inc=1, device_id=device, device_id_type=MESH)

    load_panel.wait()
    scale = 1.0 / row_total
    parts = slices(panel[...])
    lead, second, third = gram_parts(parts)
    high, error = two_sum(lead, second)
    error = error + third
    total = high + error
    error = error - (total - high)
    even, odd = halves(total * scale, error * scale)
    send[:, 0, :TILE, :] = even
    send[:, 1, :TILE, :] = odd

    load_trail.wait()
    values = trail[...]
    t0 = values.astype(bf16)
    values = values - t0.astype(f32)
    t1 = values.astype(bf16)
    t2 = (values - t1.astype(f32)).astype(bf16)
    tn = ((0,), (0,))
    both = contract(parts[0], jnp.concatenate([t0, t1, t2], axis=1), tn, None)
    more = contract(parts[1], jnp.concatenate([t0, t1], axis=1), tn, None)
    last = contract(parts[2], t0, tn, None)
    cross = both[:, :TRAIL] + (
        (both[:, TRAIL : 2 * TRAIL] + more[:, :TRAIL])
        + (both[:, 2 * TRAIL :] + more[:, TRAIL:] + last)
    )
    cross = cross * scale
    even, odd = halves(cross[:, :ORDER], cross[:, ORDER:])
    send[:, 0, TILE:, :] = even
    send[:, 1, TILE:, :] = odd

    pl.semaphore_wait(barrier, len(along) + len(around))

    for slot, (target, device) in enumerate(around):
        pltpu.make_async_remote_copy(
            src_ref=send.at[target // NC, target % NC],
            dst_ref=rs_in.at[slot],
            send_sem=rs_send,
            recv_sem=rs_recv,
            device_id=device,
            device_id_type=MESH,
        ).start()
    pltpu.make_async_copy(rs_in, rs_in, rs_recv).wait()
    terms = [send[share // NC, share % NC]] + [rs_in[k] for k in range(SHARES - 1)]
    pair, plain = add_up(terms, core)
    z_out[:TILE] = pair
    z_out[TILE:] = plain

    for device in along:
        pltpu.make_async_remote_copy(
            src_ref=z_out,
            dst_ref=z_in.at[z],
            send_sem=z_send,
            recv_sem=z_recv,
            device_id=device,
            device_id_type=MESH,
        ).start()
    z_in[z] = z_out[...]
    pltpu.make_async_copy(z_in.at[pl.ds(0, nz - 1)], z_in.at[pl.ds(0, nz - 1)], z_recv).wait()
    pair, plain = add_up([z_in[k] for k in range(nz)], core)
    gathered[share, :TILE] = pair
    gathered[share, TILE:] = plain

    for _, device in around:
        pltpu.make_async_remote_copy(
            src_ref=gathered.at[share],
            dst_ref=gathered.at[share],
            send_sem=ag_send,
            recv_sem=ag_recv,
            device_id=device,
            device_id_type=MESH,
        ).start()
    some = gathered.at[pl.ds(0, SHARES - 1)]
    pltpu.make_async_copy(some, some, ag_recv).wait()

    blocks = gathered[...].reshape(SHARES // 2, 2, 2 * TILE, ORDER)
    high, low = unhalve(blocks[:, 0, :TILE], blocks[:, 1, :TILE])
    high_ref[...] = high
    low_ref[...] = low
    left, right = unhalve(blocks[:, 0, TILE:], blocks[:, 1, TILE:])
    cross_ref[:, :ORDER] = left
    cross_ref[:, ORDER:] = right

    pltpu.make_async_copy(rs_in, rs_in, rs_send).wait()
    pltpu.make_async_copy(z_in.at[pl.ds(0, nz - 1)], z_in.at[pl.ds(0, nz - 1)], z_send).wait()
    pltpu.make_async_copy(some, some, ag_send).wait()


def reduced(panel, trailing, nz, row_total):
    rows = panel.shape[0]
    block = (2 * TILE, ORDER)
    vmem = pl.BlockSpec(memory_space=pltpu.VMEM)
    square = jax.ShapeDtypeStruct((ORDER, ORDER), f32)
    dma = pltpu.SemaphoreType.DMA
    return pl.pallas_call(
        functools.partial(reduce_kernel, nz, row_total),
        out_shape=[square, square, jax.ShapeDtypeStruct((ORDER, TRAIL), f32)],
        in_specs=[pl.BlockSpec(memory_space=pltpu.HBM)] * 2,
        out_specs=[vmem] * 3,
        scratch_shapes=[
            pltpu.VMEM((rows, ORDER), f32),
            pltpu.VMEM((rows, TRAIL), f32),
            pltpu.VMEM((SHARES // 2, 2) + block, f32),
            pltpu.VMEM((SHARES - 1,) + block, f32),
            pltpu.VMEM(block, f32),
            pltpu.VMEM((nz,) + block, f32),
            pltpu.VMEM((SHARES,) + block, f32),
            dma((2,)),
            dma, dma, dma, dma, dma, dma,
        ],
        compiler_params=pltpu.CompilerParams(
            collective_id=0, has_side_effects=True, vmem_limit_bytes=62 * 2**20
        ),
        name="reduce_grams",
    )(panel, trailing)


def apply_kernel(
    high_ref, low_ref, cross_ref, panel_ref, trail_ref, q_ref, r_ref, p_ref, u_ref,
    panel, trail, q_out, u_out, load_sem, store_sem,
):
    load_panel = pltpu.make_async_copy(panel_ref, panel, load_sem.at[0])
    load_trail = pltpu.make_async_copy(trail_ref, trail, load_sem.at[1])
    load_panel.start()
    load_trail.start()
    nn, nt = ((1,), (0,)), ((1,), (1,))
    high = high_ref[...]
    first_factor, first_inverse = factor(high)
    lead, second, third = gram_parts(slices(first_factor))
    rest, error = two_sum(high, -lead)
    rest, more = two_sum(rest, -second)
    gap = rest + ((error + more) + (low_ref[...] - third))
    eye = lax.broadcasted_iota(jnp.int32, gap.shape, 0) == lax.broadcasted_iota(
        jnp.int32, gap.shape, 1
    )
    eye = jnp.where(eye, 1.0, 0.0).astype(f32)
    gap = contract(contract(first_inverse, gap, nn), first_inverse, nt)
    gram_second = eye + gap
    second_factor, second_inverse = factor(gram_second)
    r_factor = contract(second_factor, first_factor, nn)
    r_ref[...] = r_factor
    inverse = contract(second_inverse, first_inverse, nn)
    inverse = inverse + contract(eye - contract(inverse, r_factor, nt), inverse, nn)
    projection = contract(inverse, cross_ref[...], nn)
    p_ref[...] = projection
    load_panel.wait()
    q_factor = contract(panel[...], inverse, nt)
    q_out[...] = q_factor
    store_q = pltpu.make_async_copy(q_out, q_ref, store_sem.at[0])
    store_q.start()
    load_trail.wait()
    u_out[...] = trail[...] - contract(q_factor, projection, nn)
    store_u = pltpu.make_async_copy(u_out, u_ref, store_sem.at[1])
    store_u.start()
    store_q.wait()
    store_u.wait()


def applied(high, low, cross, panel, trailing):
    rows = panel.shape[0]
    vmem = pl.BlockSpec(memory_space=pltpu.VMEM)
    hbm = pl.BlockSpec(memory_space=pltpu.HBM)
    dma = pltpu.SemaphoreType.DMA
    return pl.pallas_call(
        apply_kernel,
        out_shape=[
            jax.ShapeDtypeStruct((rows, ORDER), f32),
            jax.ShapeDtypeStruct((ORDER, ORDER), f32),
            jax.ShapeDtypeStruct((ORDER, TRAIL), f32),
            jax.ShapeDtypeStruct((rows, TRAIL), f32),
        ],
        in_specs=[vmem] * 3 + [hbm] * 2,
        out_specs=[hbm, vmem, vmem, hbm],
        scratch_shapes=[
            pltpu.VMEM((rows, ORDER), f32),
            pltpu.VMEM((rows, TRAIL), f32),
            pltpu.VMEM((rows, ORDER), f32),
            pltpu.VMEM((rows, TRAIL), f32),
            dma((2,)),
            dma((2,)),
        ],
        compiler_params=pltpu.CompilerParams(vmem_limit_bytes=62 * 2**20),
        name="factor_and_apply",
    )(high, low, cross, panel, trailing)


def solution(mesh):
    nz = mesh.shape["wide"] // (NY * NC)

    def on_device(panel, trailing):
        row_total = float(panel.shape[0] * mesh.size)
        high, low, cross = reduced(panel, trailing, nz, row_total)
        q_factor, r_factor, projection, updated = applied(high, low, cross, panel, trailing)
        return q_factor, r_factor, projection, updated

    rows = P(("wide", "narrow"), None)
    return jax.shard_map(
        on_device, mesh=mesh, in_specs=(rows, rows), out_specs=(rows, P(), P(), rows),
        check_vma=False,
    )
```

time: 1450 us -> 42.1 us (0.03)
  waiting for transfers between devices: 488 us -> 0 us
  local copies, waits for them, and re-layouts: 401 us -> 0 us
  matrix products: 313 us -> 0 us
  loops' own time: 202 us -> 0 us
  Pallas kernels: 0 us -> 41.3 us
  other arithmetic: 26.6 us -> 0 us
    psum x2 -> x0, waiting for transfers between devices: 488 us -> none  [the longest x1 245 us: on_device(): lax.psum((gram_local, cross_local), ('wide', 'narrow'))]
    dynamic_slice x640 -> x0, local copies, waits for them, and re-layouts: 377 us -> none  [the longest x384 226 us: row_step(): pivot = lax.dynamic_index_in_dim(upper_row, where, 0, keepdims=False)]
    dot_general x392 -> x0, matrix products: 313 us -> none  [the longest x384 306 us: row_step(): partial_value = jnp.dot(upper_row, inverse, precision=lax.Precision.HIGHEST)]
    another operation x5 -> x0, loops' own time: 202 us -> none  [the longest x2 190 us: upper_factor(): return lax.fori_loop(0, order, column_step, start)[1]]
    pallas_call x0 -> x2, Pallas kernels: none -> 41.3 us  [the longest x1 27.7 us: reduced(): pl.pallas_call(functools.partial(reduce_kernel, nz, row_total), out_shape...]
    dynamic_update_slice x640 -> x0, local copies, waits for them, and re-layouts: 21.3 us -> none  [the longest x384 11.7 us: row_step(): return lax.dynamic_update_slice_in_dim(inverse, new_row[None, :], where, 0)]
    sub x256 -> x0, other arithmetic: 21 us -> none  [column_step(): work = work - new_row[:, None] * new_row[None, :]]
  transfers between devices with their start and end apart: 2 -> 0, of which waited for: 2 -> 0; matrix products, arithmetic and copies ran while one was open for 0% -> 0% of each run, Pallas kernels for 0% -> 0%
where the time goes in v1:
time: 42.1 us; the launch traced here: 42 us
  Pallas kernels  41.3 us (98%)
  between operations  0.64 us (2%)
    pallas_call x1, Pallas kernels, reduced(): pl.pallas_call(functools.partial(reduce_kernel, nz, row_total), out_shape...  27.7 us
    pallas_call x1, Pallas kernels, applied(): pl.pallas_call(apply_kernel, out_shape=[jax.ShapeDtypeStruct((rows, ORDER...  13.6 us

profile of v1, /device:TPU:1, one launch (start us, length us, event | category | flops | bytes accessed | tf_op | source)
XLA Modules:
  0.0 42.0 jit_solution(15681975509234541838)
XLA Ops:
  0.6 27.7 %reduce_grams.1 = (f32[128,128]{1,0:T(8,128)}, f32[128,128]{1,0:T(8,128)}, f32[128,256]{1,0:T(8,128)}) custom-call(f32[512,128]{1,0:T(8,128)} %panel_ref.3, f32[512,256]{1,0:T(8,128)} %trail_ref.3), custom_call_target="tpu_custom_call" | custom-call | tf_op jit(solution)/shard_map/reduce_grams/pallas_call | solution.py:266
  28.4 13.6 %factor_and_apply.1 = (f32[512,128]{1,0:T(8,128)}, f32[128,128]{1,0:T(8,128)}, f32[128,256]{1,0:T(8,128)}, f32[512,256]{1,0:T(8,128)}) custom-call(f32[128,128]{1,0:T(8,128)} %get-tuple-element.7.high_ref, f32[128,128]{1,0:T(8,128)} %get-tuple-element.8.low_ref, f32[128,256]{1,0:T(8,128)} %get-tuple-element.9.cross_ref, f32[512,128]{1,0:T(8,128)} %panel_ref.3, ...), custom_call_target="tpu_custom_call" | custom-call | tf_op jit(solution)/shard_map/factor_and_apply/pallas_call | solution.py:335

commit v2 on v1

--- a/solution.py
+++ b/solution.py
@@ -80,7 +80,7 @@
             pivot = column[0, i : i + 1, :]
             pivots = jnp.where(sub == i, pivot, pivots)
             if i + 1 < width:
-                ratio = jnp.where(sub > i, column[0] * (1.0 / pivot), 0.0)
+                ratio = jnp.where(sub > i, column[0], 0.0) * (1.0 / pivot)
                 column = column[1:] - ratio[None] * column[1:, i : i + 1, :]
                 top = top - ratio * top[i : i + 1, :]
                 top_inverse = top_inverse - ratio * top_inverse[i : i + 1, :]
@@ -115,27 +115,29 @@
     return left.reshape(ORDER, ORDER), right.reshape(ORDER, ORDER)
 
 
-def add_up(terms, core):
+def add_pairs(terms, core):
     sub = lax.broadcasted_iota(jnp.int32, (TILE, ORDER), 0)
     mine = (sub // 4) == core
-    total, error = terms[0][:TILE], jnp.zeros((TILE, ORDER), f32)
-    plain = [t[TILE:] for t in terms]
+    total, error = terms[0], jnp.zeros((TILE, ORDER), f32)
     for term in terms[1:]:
-        total, more = two_sum(total, term[:TILE])
+        total, more = two_sum(total, term)
         error = error + more
     low = error + swap(total + error)
     high = total + low
-    rest = low - (high - total)
-    while len(plain) > 1:
-        plain = [a + b for a, b in zip(plain[::2], plain[1::2])] + (
-            [plain[-1]] if len(plain) % 2 else []
+    return jnp.where(mine, high, swap(low - (high - total)))
+
+
+def add_plain(terms):
+    while len(terms) > 1:
+        terms = [a + b for a, b in zip(terms[::2], terms[1::2])] + (
+            [terms[-1]] if len(terms) % 2 else []
         )
-    return jnp.where(mine, high, swap(rest)), plain[0]
+    return terms[0]
 
 
 def reduce_kernel(
     nz, row_total,
-    panel_ref, trail_ref, high_ref, low_ref, cross_ref,
+    panel_ref, trail_ref, factor_ref, inverse_ref, gap_ref, cross_ref,
     panel, trail, send, rs_in, z_out, z_in, gathered,
     load_sem, rs_send, rs_recv, z_send, z_recv, ag_send, ag_recv,
 ):
@@ -169,6 +171,53 @@
     for device in along + [device for _, device in around]:
         pl.semaphore_signal(barrier, inc=1, device_id=device, device_id_type=MESH)
 
+    def copy(src, dst, send_sem, recv_sem, device):
+        pltpu.make_async_remote_copy(
+            src_ref=src, dst_ref=dst, send_sem=send_sem, recv_sem=recv_sem,
+            device_id=device, device_id_type=MESH,
+        ).start()
+
+    def scatter(k):
+        for slot, (target, device) in enumerate(around):
+            copy(
+                send.at[k, target // NC, target % NC], rs_in.at[k, slot],
+                rs_send.at[k], rs_recv.at[k], device,
+            )
+
+    def scattered(k):
+        pltpu.make_async_copy(rs_in.at[k], rs_in.at[k], rs_recv.at[k]).wait()
+        return [send[k, share // NC, share % NC]] + [rs_in[k, n] for n in range(SHARES - 1)]
+
+    def exchange(k, block):
+        z_out[k] = block
+        for device in along:
+            copy(z_out.at[k], z_in.at[k, z], z_send.at[k], z_recv.at[k], device)
+        z_in[k, z] = block
+
+    def exchanged(k):
+        others = z_in.at[k, pl.ds(0, nz - 1)]
+        pltpu.make_async_copy(others, others, z_recv.at[k]).wait()
+        return [z_in[k, n] for n in range(nz)]
+
+    def gather(k, block):
+        gathered[k, share] = block
+        for _, device in around:
+            copy(
+                gathered.at[k, share], gathered.at[k, share],
+                ag_send.at[k], ag_recv.at[k], device,
+            )
+
+    def gathered_pair(k):
+        others = gathered.at[k, pl.ds(0, SHARES - 1)]
+        pltpu.make_async_copy(others, others, ag_recv.at[k]).wait()
+        blocks = gathered[k].reshape(SHARES // NC, NC, TILE, ORDER)
+        return unhalve(blocks[:, 0], blocks[:, 1])
+
+    def stage(k, left, right):
+        even, odd = halves(left, right)
+        send[k, :, 0] = even
+        send[k, :, 1] = odd
+
     load_panel.wait()
     scale = 1.0 / row_total
     parts = slices(panel[...])
@@ -177,9 +226,10 @@
     error = error + third
     total = high + error
     error = error - (total - high)
-    even, odd = halves(total * scale, error * scale)
-    send[:, 0, :TILE, :] = even
-    send[:, 1, :TILE, :] = odd
+    stage(0, total * scale, error * scale)
+
+    pl.semaphore_wait(barrier, len(along) + len(around))
+    scatter(0)
 
     load_trail.wait()
     values = trail[...]
@@ -196,122 +246,100 @@
         + (both[:, 2 * TRAIL :] + more[:, TRAIL:] + last)
     )
     cross = cross * scale
-    even, odd = halves(cross[:, :ORDER], cross[:, ORDER:])
-    send[:, 0, TILE:, :] = even
-    send[:, 1, TILE:, :] = odd
-
-    pl.semaphore_wait(barrier, len(along) + len(around))
-
-    for slot, (target, device) in enumerate(around):
-        pltpu.make_async_remote_copy(
-            src_ref=send.at[target // NC, target % NC],
-            dst_ref=rs_in.at[slot],
-            send_sem=rs_send,
-            recv_sem=rs_recv,
-            device_id=device,
-            device_id_type=MESH,
-        ).start()
-    pltpu.make_async_copy(rs_in, rs_in, rs_recv).wait()
-    terms = [send[share // NC, share % NC]] + [rs_in[k] for k in range(SHARES - 1)]
-    pair, plain = add_up(terms, core)
-    z_out[:TILE] = pair
-    z_out[TILE:] = plain
-
-    for device in along:
-        pltpu.make_async_remote_copy(
-            src_ref=z_out,
-            dst_ref=z_in.at[z],
-            send_sem=z_send,
-            recv_sem=z_recv,
-            device_id=device,
-            device_id_type=MESH,
-        ).start()
-    z_in[z] = z_out[...]
-    pltpu.make_async_copy(z_in.at[pl.ds(0, nz - 1)], z_in.at[pl.ds(0, nz - 1)], z_recv).wait()
-    pair, plain = add_up([z_in[k] for k in range(nz)], core)
-    gathered[share, :TILE] = pair
-    gathered[share, TILE:] = plain
-
-    for _, device in around:
-        pltpu.make_async_remote_copy(
-            src_ref=gathered.at[share],
-            dst_ref=gathered.at[share],
-            send_sem=ag_send,
-            recv_sem=ag_recv,
-            device_id=device,
-            device_id_type=MESH,
-        ).start()
-    some = gathered.at[pl.ds(0, SHARES - 1)]
-    pltpu.make_async_copy(some, some, ag_recv).wait()
-
-    blocks = gathered[...].reshape(SHARES // 2, 2, 2 * TILE, ORDER)
-    high, low = unhalve(blocks[:, 0, :TILE], blocks[:, 1, :TILE])
-    high_ref[...] = high
-    low_ref[...] = low
-    left, right = unhalve(blocks[:, 0, TILE:], blocks[:, 1, TILE:])
+    stage(1, cross[:, :ORDER], cross[:, ORDER:])
+    scatter(1)
+
+    exchange(0, add_pairs(scattered(0), core))
+    exchange(1, add_plain(scattered(1)))
+    gather(0, add_pairs(exchanged(0), core))
+    gather(1, add_plain(exchanged(1)))
+    high, low = gathered_pair(0)
+
+    nn, nt = ((1,), (0,)), ((1,), (1,))
+    first_factor, first_inverse = factor(high)
+    factor_ref[...] = first_factor
+    inverse_ref[...] = first_inverse
+    lead, second, third = gram_parts(slices(first_factor))
+    rest, error = two_sum(high, -lead)
+    rest, more = two_sum(rest, -second)
+    gap = rest + ((error + more) + (low - third))
+    gap_ref[...] = contract(contract(first_inverse, gap, nn), first_inverse, nt)
+
+    left, right = gathered_pair(1)
     cross_ref[:, :ORDER] = left
     cross_ref[:, ORDER:] = right
 
-    pltpu.make_async_copy(rs_in, rs_in, rs_send).wait()
-    pltpu.make_async_copy(z_in.at[pl.ds(0, nz - 1)], z_in.at[pl.ds(0, nz - 1)], z_send).wait()
-    pltpu.make_async_copy(some, some, ag_send).wait()
+    for k in range(2):
+        pltpu.make_async_copy(rs_in.at[k], rs_in.at[k], rs_send.at[k]).wait()
+        others = z_in.at[k, pl.ds(0, nz - 1)]
+        pltpu.make_async_copy(others, others, z_send.at[k]).wait()
+        others = gathered.at[k, pl.ds(0, SHARES - 1)]
+        pltpu.make_async_copy(others, others, ag_send.at[k]).wait()
 
 
 def reduced(panel, trailing, nz, row_total):
     rows = panel.shape[0]
-    block = (2 * TILE, ORDER)
+    block = (TILE, ORDER)
     vmem = pl.BlockSpec(memory_space=pltpu.VMEM)
     square = jax.ShapeDtypeStruct((ORDER, ORDER), f32)
     dma = pltpu.SemaphoreType.DMA
     return pl.pallas_call(
         functools.partial(reduce_kernel, nz, row_total),
-        out_shape=[square, square, jax.ShapeDtypeStruct((ORDER, TRAIL), f32)],
+        out_shape=[square, square, square, jax.ShapeDtypeStruct((ORDER, TRAIL), f32)],
         in_specs=[pl.BlockSpec(memory_space=pltpu.HBM)] * 2,
-        out_specs=[vmem] * 3,
+        out_specs=[vmem] * 4,
         scratch_shapes=[
             pltpu.VMEM((rows, ORDER), f32),
             pltpu.VMEM((rows, TRAIL), f32),
-            pltpu.VMEM((SHARES // 2, 2) + block, f32),
-            pltpu.VMEM((SHARES - 1,) + block, f32),
-            pltpu.VMEM(block, f32),
-            pltpu.VMEM((nz,) + block, f32),
-            pltpu.VMEM((SHARES,) + block, f32),
-            dma((2,)),
-            dma, dma, dma, dma, dma, dma,
-        ],
+            pltpu.VMEM((2, SHARES // NC, NC) + block, f32),
+            pltpu.VMEM((2, SHARES - 1) + block, f32),
+            pltpu.VMEM((2,) + block, f32),
+            pltpu.VMEM((2, nz) + block, f32),
+            pltpu.VMEM((2, SHARES) + block, f32),
+        ]
+        + [dma((2,))] * 7,
         compiler_params=pltpu.CompilerParams(
             collective_id=0, has_side_effects=True, vmem_limit_bytes=62 * 2**20
         ),
-        name="reduce_grams",
+        name="reduce_and_factor",
     )(panel, trailing)
 
 
 def apply_kernel(
-    high_ref, low_ref, cross_ref, panel_ref, trail_ref, q_ref, r_ref, p_ref, u_ref,
-    panel, trail, q_out, u_out, load_sem, store_sem,
+    factor_ref, inverse_ref, gap_ref, cross_ref, panel_ref, trail_ref,
+    q_ref, r_ref, p_ref, u_ref,
+    panel, trail, q_out, u_out, whole, load_sem, store_sem,
 ):
     load_panel = pltpu.make_async_copy(panel_ref, panel, load_sem.at[0])
     load_trail = pltpu.make_async_copy(trail_ref, trail, load_sem.at[1])
     load_panel.start()
     load_trail.start()
-    nn, nt = ((1,), (0,)), ((1,), (1,))
-    high = high_ref[...]
-    first_factor, first_inverse = factor(high)
-    lead, second, third = gram_parts(slices(first_factor))
-    rest, error = two_sum(high, -lead)
-    rest, more = two_sum(rest, -second)
-    gap = rest + ((error + more) + (low_ref[...] - third))
-    eye = lax.broadcasted_iota(jnp.int32, gap.shape, 0) == lax.broadcasted_iota(
-        jnp.int32, gap.shape, 1
-    )
-    eye = jnp.where(eye, 1.0, 0.0).astype(f32)
-    gap = contract(contract(first_inverse, gap, nn), first_inverse, nt)
-    gram_second = eye + gap
-    second_factor, second_inverse = factor(gram_second)
-    r_factor = contract(second_factor, first_factor, nn)
-    r_ref[...] = r_factor
-    inverse = contract(second_inverse, first_inverse, nn)
-    inverse = inverse + contract(eye - contract(inverse, r_factor, nt), inverse, nn)
+    nn, nt, tn = ((1,), (0,)), ((1,), (1,)), ((0,), (0,))
+    gap = gap_ref[...]
+    rows = lax.broadcasted_iota(jnp.int32, gap.shape, 0)
+    cols = lax.broadcasted_iota(jnp.int32, gap.shape, 1)
+    eye = jnp.where(rows == cols, 1.0, 0.0).astype(f32)
+    weight = jnp.where(rows < cols, 1.0, 0.5 * eye).astype(f32)
+    small = jnp.sum(gap * gap) < 2.0**-7
+
+    @pl.when(small)
+    def _():
+        first_factor, first_inverse, gap = factor_ref[...], inverse_ref[...], gap_ref[...]
+        upper = weight * gap
+        for _ in range(5):
+            upper = weight * (gap - contract(upper, upper, tn))
+        r_ref[...] = first_factor + contract(upper, first_factor, nn)
+        once = first_inverse - contract(upper, first_inverse, tn)
+        whole[...] = first_inverse - contract(upper, once, tn)
+
+    @pl.when(jnp.logical_not(small))
+    def _():
+        second_factor, second_inverse = factor(eye + gap_ref[...])
+        r_ref[...] = contract(second_factor, factor_ref[...], nn)
+        whole[...] = contract(second_inverse, inverse_ref[...], nn)
+
+    inverse = whole[...]
+    inverse = inverse + contract(eye - contract(inverse, r_ref[...], nt), inverse, nn)
     projection = contract(inverse, cross_ref[...], nn)
     p_ref[...] = projection
     load_panel.wait()
@@ -327,7 +355,7 @@
     store_u.wait()
 
 
-def applied(high, low, cross, panel, trailing):
+def applied(first_factor, first_inverse, gap, cross, panel, trailing):
     rows = panel.shape[0]
     vmem = pl.BlockSpec(memory_space=pltpu.VMEM)
     hbm = pl.BlockSpec(memory_space=pltpu.HBM)
@@ -340,19 +368,20 @@
             jax.ShapeDtypeStruct((ORDER, TRAIL), f32),
             jax.ShapeDtypeStruct((rows, TRAIL), f32),
         ],
-        in_specs=[vmem] * 3 + [hbm] * 2,
+        in_specs=[vmem] * 4 + [hbm] * 2,
         out_specs=[hbm, vmem, vmem, hbm],
         scratch_shapes=[
             pltpu.VMEM((rows, ORDER), f32),
             pltpu.VMEM((rows, TRAIL), f32),
             pltpu.VMEM((rows, ORDER), f32),
             pltpu.VMEM((rows, TRAIL), f32),
+            pltpu.VMEM((ORDER, ORDER), f32),
             dma((2,)),
             dma((2,)),
         ],
         compiler_params=pltpu.CompilerParams(vmem_limit_bytes=62 * 2**20),
-        name="factor_and_apply",
-    )(high, low, cross, panel, trailing)
+        name="apply_factor",
+    )(first_factor, first_inverse, gap, cross, panel, trailing)
 
 
 def solution(mesh):
@@ -360,8 +389,8 @@
 
     def on_device(panel, trailing):
         row_total = float(panel.shape[0] * mesh.size)
-        high, low, cross = reduced(panel, trailing, nz, row_total)
-        q_factor, r_factor, projection, updated = applied(high, low, cross, panel, trailing)
+        parts = reduced(panel, trailing, nz, row_total)
+        q_factor, r_factor, projection, updated = applied(*parts, panel, trailing)
         return q_factor, r_factor, projection, updated
 
     rows = P(("wide", "narrow"), None)

time: 42.1 us -> 39.4 us (0.936)
  Pallas kernels: 41.3 us -> 38.7 us
    pallas_call x1, Pallas kernels: 13.6 us -> 6.75 us  [applied(): pl.pallas_call(apply_kernel, out_shape=[jax.ShapeDtypeStruct((rows, ORDER...]
    pallas_call x1, Pallas kernels: 27.7 us -> 31.9 us  [reduced(): pl.pallas_call(functools.partial(reduce_kernel, nz, row_total), out_shape...]
where the time goes in v2:
time: 39.4 us; the launch traced here: 39.3 us
  Pallas kernels  38.7 us (98%)
  between operations  0.64 us (2%)
    pallas_call x1, Pallas kernels, reduced(): pl.pallas_call(functools.partial(reduce_kernel, nz, row_total), out_shape...  31.9 us
    pallas_call x1, Pallas kernels, applied(): pl.pallas_call(apply_kernel, out_shape=[jax.ShapeDtypeStruct((rows, ORDER...  6.75 us

profile of v2, /device:TPU:1, one launch (start us, length us, event | category | flops | bytes accessed | tf_op | source)
XLA Modules:
  0.0 39.3 jit_solution(9446751383623190529)
XLA Ops:
  0.6 31.9 %reduce_and_factor.1 = (f32[128,128]{1,0:T(8,128)}, f32[128,128]{1,0:T(8,128)}, f32[128,128]{1,0:T(8,128)}, f32[128,256]{1,0:T(8,128)}) custom-call(f32[512,128]{1,0:T(8,128)} %panel_ref.3, f32[512,256]{1,0:T(8,128)} %trail_ref.3), custom_call_target="tpu_custom_call" | custom-call | tf_op jit(solution)/shard_map/reduce_and_factor/pallas_call | solution.py:286
  32.6 6.7 %apply_factor.1 = (f32[512,128]{1,0:T(8,128)}, f32[128,128]{1,0:T(8,128)}, f32[128,256]{1,0:T(8,128)}, f32[512,256]{1,0:T(8,128)}) custom-call(f32[128,128]{1,0:T(8,128)} %get-tuple-element.8.factor_ref, f32[128,128]{1,0:T(8,128)} %get-tuple-element.9.inverse_ref, f32[128,128]{1,0:T(8,128)} %get-tuple-element.10.gap_ref, ...), custom_call_target="tpu_custom_call" | custom-call | tf_op jit(solution)/shard_map/apply_factor/pallas_call | solution.py:363

commit v3 on v2

--- a/solution.py
+++ b/solution.py
@@ -17,7 +17,8 @@
 NX, NY, NC = 4, 4, 2
 SHARES = NX * NY * NC
 TILE = 8
-WIDTH = 32
+WIDTH = 16
+CHUNKS = 2
 
 
 def contract(left, right, dims, precision=HIGHEST):
@@ -59,6 +60,15 @@
     return first[:, :n], cross + cross.T, (tail + tail.T) + (second[:, :n] + third)
 
 
+def split(values, count=3):
+    parts = []
+    for _ in range(count - 1):
+        part = values.astype(bf16)
+        values = values - part.astype(f32)
+        parts.append(part)
+    return parts + [values.astype(bf16)]
+
+
 def factor(work):
     order, width = work.shape[0], WIDTH
     rows = lax.broadcasted_iota(jnp.int32, (order, order), 0)
@@ -66,6 +76,7 @@
     inverse = jnp.where(rows == cols, 1.0, 0.0).astype(f32)
     sub = lax.broadcasted_iota(jnp.int32, (width, order), 0)
     lane = lax.broadcasted_iota(jnp.int32, (width, order), 1)
+    row = lax.broadcasted_iota(jnp.int32, (TILE, order), 0)
     uppers, inverses = [], []
     for start in range(0, order, width):
         top, top_inverse = work[:width], inverse[:width]
@@ -75,26 +86,64 @@
                 for k in range(width)
             ]
         )
-        pivots = jnp.ones((width, order), f32)
+        done, done_inverse, pivots = [], [], []
         for i in range(width):
-            pivot = column[0, i : i + 1, :]
-            pivots = jnp.where(sub == i, pivot, pivots)
+            r = i % TILE
+            pivot = column[0, r : r + 1, :]
+            held = pivot if r == 0 else jnp.where(row == r, pivot, held)
             if i + 1 < width:
-                ratio = jnp.where(sub > i, column[0], 0.0) * (1.0 / pivot)
-                column = column[1:] - ratio[None] * column[1:, i : i + 1, :]
-                top = top - ratio * top[i : i + 1, :]
-                top_inverse = top_inverse - ratio * top_inverse[i : i + 1, :]
-        scale = lax.rsqrt(pivots)
-        upper = jnp.where(sub + start <= lane, top * scale, 0.0)
-        lower = top_inverse * scale
-        uppers.append(upper)
+                below = jnp.where(row > r, column[0, :TILE], 0.0)
+                if column.shape[1] > TILE:
+                    below = jnp.concatenate([below, column[0, TILE:]], axis=0)
+                ratio = below * (1.0 / pivot)
+                column = column[1:] - ratio[None] * column[1:, r : r + 1, :]
+                top = top - ratio * top[r : r + 1, :]
+                top_inverse = top_inverse - ratio * top_inverse[r : r + 1, :]
+            if r == TILE - 1:
+                done.append(top[:TILE])
+                done_inverse.append(top_inverse[:TILE])
+                pivots.append(held)
+                if i + 1 < width:
+                    top, top_inverse, column = top[TILE:], top_inverse[TILE:], column[:, TILE:]
+        scale = lax.rsqrt(jnp.concatenate(pivots, axis=0))
+        upper = jnp.concatenate(done, axis=0) * scale
+        lower = jnp.concatenate(done_inverse, axis=0) * scale
+        uppers.append(jnp.where(sub + start <= lane, upper, 0.0))
         inverses.append(lower)
         if start + width < order:
-            both = jnp.concatenate([upper, lower], axis=1)
-            step = contract(upper, both, ((0,), (0,)))[start + width :]
+            a0, a1, a2 = split(upper)
+            b0, b1, b2 = split(jnp.concatenate([upper, lower], axis=1))
+            left = jnp.concatenate([a0, a0, a1, a0, a2, a1], axis=0).T
+            right = jnp.concatenate([b0, b1, b0, b2, b0, b1], axis=0)
+            step = contract(left[start + width :], right, ((1,), (0,)), None)
             work = work[width:] - step[:, :order]
             inverse = inverse[width:] - step[:, order:]
     return jnp.concatenate(uppers, axis=0), jnp.concatenate(inverses, axis=0)
+
+
+def times_square(left, right):
+    a0, a1, a2 = left
+    b0, b1, b2 = right
+    nn = ((1,), (0,))
+    pair = jnp.concatenate([jnp.concatenate([b0, b1], axis=1)] * 2, axis=0)
+    most = contract(jnp.concatenate([a0, a1], axis=1), pair, nn, None)
+    rest = contract(
+        jnp.concatenate([a0, a2], axis=1), jnp.concatenate([b2, b0], axis=0), nn, None
+    )
+    return most[:, :ORDER] + (most[:, ORDER:] + rest)
+
+
+def times_wide(left, right):
+    a0, a1, a2 = left
+    b0, b1, b2 = right
+    nn = ((1,), (0,))
+    pair = jnp.concatenate([b0, b1], axis=0)
+    most = contract(jnp.concatenate([a0, a0], axis=1), pair, nn, None)
+    more = contract(jnp.concatenate([a1, a1], axis=1), pair, nn, None)
+    rest = contract(
+        jnp.concatenate([a0, a2], axis=1), jnp.concatenate([b2, b0], axis=0), nn, None
+    )
+    return most + (more + rest)
 
 
 def swap(tiles):
@@ -281,11 +330,10 @@
     rows = panel.shape[0]
     block = (TILE, ORDER)
     vmem = pl.BlockSpec(memory_space=pltpu.VMEM)
-    square = jax.ShapeDtypeStruct((ORDER, ORDER), f32)
     dma = pltpu.SemaphoreType.DMA
     return pl.pallas_call(
         functools.partial(reduce_kernel, nz, row_total),
-        out_shape=[square, square, square, jax.ShapeDtypeStruct((ORDER, TRAIL), f32)],
+        out_shape=[pltpu.VMEM((ORDER, ORDER), f32)] * 3 + [pltpu.VMEM((ORDER, TRAIL), f32)],
         in_specs=[pl.BlockSpec(memory_space=pltpu.HBM)] * 2,
         out_specs=[vmem] * 4,
         scratch_shapes=[
@@ -308,51 +356,59 @@
 def apply_kernel(
     factor_ref, inverse_ref, gap_ref, cross_ref, panel_ref, trail_ref,
     q_ref, r_ref, p_ref, u_ref,
-    panel, trail, q_out, u_out, whole, load_sem, store_sem,
+    q_out, u_out, whole, store_sem,
 ):
-    load_panel = pltpu.make_async_copy(panel_ref, panel, load_sem.at[0])
-    load_trail = pltpu.make_async_copy(trail_ref, trail, load_sem.at[1])
-    load_panel.start()
-    load_trail.start()
     nn, nt, tn = ((1,), (0,)), ((1,), (1,)), ((0,), (0,))
     gap = gap_ref[...]
     rows = lax.broadcasted_iota(jnp.int32, gap.shape, 0)
     cols = lax.broadcasted_iota(jnp.int32, gap.shape, 1)
     eye = jnp.where(rows == cols, 1.0, 0.0).astype(f32)
     weight = jnp.where(rows < cols, 1.0, 0.5 * eye).astype(f32)
-    small = jnp.sum(gap * gap) < 2.0**-7
+    small = jnp.sum(gap * gap) < 0.01
 
     @pl.when(small)
     def _():
         first_factor, first_inverse, gap = factor_ref[...], inverse_ref[...], gap_ref[...]
         upper = weight * gap
-        for _ in range(5):
+        close = None
+        for step in range(4):
             upper = weight * (gap - contract(upper, upper, tn))
+            if step == 1:
+                close = upper
+        once = first_inverse - contract(close, first_inverse, tn)
+        guess = first_inverse - contract(close, once, tn)
+        left = contract(guess, first_factor, nt)
+        rough = contract(guess, cross_ref[...], nn)
         r_ref[...] = first_factor + contract(upper, first_factor, nn)
-        once = first_inverse - contract(upper, first_inverse, tn)
-        whole[...] = first_inverse - contract(upper, once, tn)
+        rest = (eye - left) - contract(left, upper, nt)
+        turned = guess.T
+        whole[...] = turned + contract(turned, rest, nt)
+        p_ref[...] = rough + contract(rest, rough, nn)
 
     @pl.when(jnp.logical_not(small))
     def _():
         second_factor, second_inverse = factor(eye + gap_ref[...])
-        r_ref[...] = contract(second_factor, factor_ref[...], nn)
-        whole[...] = contract(second_inverse, inverse_ref[...], nn)
-
-    inverse = whole[...]
-    inverse = inverse + contract(eye - contract(inverse, r_ref[...], nt), inverse, nn)
-    projection = contract(inverse, cross_ref[...], nn)
-    p_ref[...] = projection
-    load_panel.wait()
-    q_factor = contract(panel[...], inverse, nt)
-    q_out[...] = q_factor
-    store_q = pltpu.make_async_copy(q_out, q_ref, store_sem.at[0])
-    store_q.start()
-    load_trail.wait()
-    u_out[...] = trail[...] - contract(q_factor, projection, nn)
-    store_u = pltpu.make_async_copy(u_out, u_ref, store_sem.at[1])
-    store_u.start()
-    store_q.wait()
-    store_u.wait()
+        r_factor = contract(second_factor, factor_ref[...], nn)
+        r_ref[...] = r_factor
+        guess = contract(second_inverse, inverse_ref[...], nn)
+        inverse = guess + contract(eye - contract(guess, r_factor, nt), guess, nn)
+        whole[...] = inverse.T
+        p_ref[...] = contract(inverse, cross_ref[...], nn)
+
+    inverse, projection = split(whole[...]), split(p_ref[...])
+    size = panel_ref.shape[0] // CHUNKS
+    stores = []
+    for k in range(CHUNKS):
+        part = pl.ds(k * size, size)
+        q_factor = times_square(split(panel_ref[part]), inverse)
+        q_out[part] = q_factor
+        stores.append(pltpu.make_async_copy(q_out.at[part], q_ref.at[part], store_sem.at[0, k]))
+        stores[-1].start()
+        u_out[part] = trail_ref[part] - times_wide(split(q_factor), projection)
+        stores.append(pltpu.make_async_copy(u_out.at[part], u_ref.at[part], store_sem.at[1, k]))
+        stores[-1].start()
+    for store in stores:
+        store.wait()
 
 
 def applied(first_factor, first_inverse, gap, cross, panel, trailing):
@@ -368,18 +424,15 @@
             jax.ShapeDtypeStruct((ORDER, TRAIL), f32),
             jax.ShapeDtypeStruct((rows, TRAIL), f32),
         ],
-        in_specs=[vmem] * 4 + [hbm] * 2,
+        in_specs=[vmem] * 6,
         out_specs=[hbm, vmem, vmem, hbm],
         scratch_shapes=[
             pltpu.VMEM((rows, ORDER), f32),
             pltpu.VMEM((rows, TRAIL), f32),
-            pltpu.VMEM((rows, ORDER), f32),
-            pltpu.VMEM((rows, TRAIL), f32),
             pltpu.VMEM((ORDER, ORDER), f32),
-            dma((2,)),
-            dma((2,)),
+            dma((2, CHUNKS)),
         ],
-        compiler_params=pltpu.CompilerParams(vmem_limit_bytes=62 * 2**20),
+        compiler_params=pltpu.CompilerParams(vmem_limit_bytes=32 * 2**20),
         name="apply_factor",
     )(first_factor, first_inverse, gap, cross, panel, trailing)
 

time: 39.4 us -> 35.6 us (0.904)
  Pallas kernels: 38.7 us -> 34.8 us
    pallas_call x1, Pallas kernels: 6.75 us -> 4.52 us  [applied(): pl.pallas_call(apply_kernel, out_shape=[jax.ShapeDtypeStruct((rows, ORDER...]
    pallas_call x1, Pallas kernels: 31.9 us -> 30.3 us  [reduced(): pl.pallas_call(functools.partial(reduce_kernel, nz, row_total), out_shape...]
where the time goes in v3:
time: 35.6 us; the launch traced here: 35.5 us
  Pallas kernels  34.8 us (98%)
  between operations  0.67 us (2%)
    pallas_call x1, Pallas kernels, reduced(): pl.pallas_call(functools.partial(reduce_kernel, nz, row_total), out_shape...  30.3 us
    pallas_call x1, Pallas kernels, applied(): pl.pallas_call(apply_kernel, out_shape=[jax.ShapeDtypeStruct((rows, ORDER...  4.52 us

profile of v3, /device:TPU:1, one launch (start us, length us, event | category | flops | bytes accessed | tf_op | source)
XLA Modules:
  0.0 35.5 jit_solution(13122831867889728681)
XLA Ops:
  0.6 0.0 copy-start
  0.6 0.0 copy-start.1
  0.7 30.3 %reduce_and_factor.1 = (f32[128,128]{1,0:T(8,128)S(1)}, f32[128,128]{1,0:T(8,128)S(1)}, f32[128,128]{1,0:T(8,128)S(1)}, f32[128,256]{1,0:T(8,128)S(1)}) custom-call(f32[512,128]{1,0:T(8,128)} %panel_ref.3, f32[512,256]{1,0:T(8,128)} %trail_ref.3), custom_call_target="tpu_custom_call" | custom-call | tf_op jit(solution)/shard_map/reduce_and_factor/pallas_call | solution.py:334
  30.9 0.0 copy-done
  30.9 0.0 copy-done.1
  30.9 4.5 %apply_factor.1 = (f32[512,128]{1,0:T(8,128)}, f32[128,128]{1,0:T(8,128)}, f32[128,256]{1,0:T(8,128)}, f32[512,256]{1,0:T(8,128)}) custom-call(f32[128,128]{1,0:T(8,128)S(1)} %get-tuple-element.8.factor_ref, f32[128,128]{1,0:T(8,128)S(1)} %get-tuple-element.9.inverse_ref, f32[128,128]{1,0:T(8,128)S(1)} %get-tuple-element.10.gap_ref, ...), custom_call_target="tpu_custom_call" | custom-call | tf_op jit(solution)/shard_map/apply_factor/pallas_call | solution.py:419
Async XLA Ops:
  0.6 30.3 %copy-start = (f32[512,256]{1,0:T(8,128)S(1)}, f32[512,256]{1,0:T(8,128)}, u32[]{:S(2)}) copy-start(f32[512,256]{1,0:T(8,128)} %trail_ref.3) | copy-start | bytes 1572868
  0.6 30.3 %copy-start.1 = (f32[512,128]{1,0:T(8,128)S(1)}, f32[512,128]{1,0:T(8,128)}, u32[]{:S(2)}) copy-start(f32[512,128]{1,0:T(8,128)} %panel_ref.3) | copy-start | bytes 786436

commit v4 on v3

--- a/solution.py
+++ b/solution.py
@@ -19,6 +19,7 @@
 TILE = 8
 WIDTH = 16
 CHUNKS = 2
+STEPS = 3
 
 
 def contract(left, right, dims, precision=HIGHEST):
@@ -121,6 +122,19 @@
     return jnp.concatenate(uppers, axis=0), jnp.concatenate(inverses, axis=0)
 
 
+def times_close(left, right, turned=False):
+    a0, a1 = split(left, 2)
+    b0, b1 = split(right, 2)
+    sides = jnp.concatenate([a0, a1], axis=1)
+    if turned:
+        rows = jnp.concatenate([b0, b1], axis=0)
+        both = contract(sides, jnp.concatenate([rows, rows], axis=1), ((1,), (1,)), None)
+    else:
+        rows = jnp.concatenate([b0, b1], axis=1)
+        both = contract(sides, jnp.concatenate([rows, rows], axis=0), ((1,), (0,)), None)
+    return both[:, :ORDER] + both[:, ORDER:]
+
+
 def times_square(left, right):
     a0, a1, a2 = left
     b0, b1, b2 = right
@@ -190,11 +204,6 @@
     panel, trail, send, rs_in, z_out, z_in, gathered,
     load_sem, rs_send, rs_recv, z_send, z_recv, ag_send, ag_recv,
 ):
-    load_panel = pltpu.make_async_copy(panel_ref, panel, load_sem.at[0])
-    load_trail = pltpu.make_async_copy(trail_ref, trail, load_sem.at[1])
-    load_panel.start()
-    load_trail.start()
-
     wide, x = lax.axis_index("wide"), lax.axis_index("narrow")
     z, y, core = wide // (NY * NC), (wide // NC) % NY, wide % NC
     share = (x * NY + y) * NC + core
@@ -217,8 +226,13 @@
     along = [((((z + d) % nz) * NY + y) * NC + core, x) for d in steps]
 
     barrier = pltpu.get_barrier_semaphore()
-    for device in along + [device for _, device in around]:
+    for device in [device for _, device in around] + along:
         pl.semaphore_signal(barrier, inc=1, device_id=device, device_id_type=MESH)
+
+    load_panel = pltpu.make_async_copy(panel_ref, panel, load_sem.at[0])
+    load_trail = pltpu.make_async_copy(trail_ref, trail, load_sem.at[1])
+    load_panel.start()
+    load_trail.start()
 
     def copy(src, dst, send_sem, recv_sem, device):
         pltpu.make_async_remote_copy(
@@ -304,7 +318,6 @@
     gather(1, add_plain(exchanged(1)))
     high, low = gathered_pair(0)
 
-    nn, nt = ((1,), (0,)), ((1,), (1,))
     first_factor, first_inverse = factor(high)
     factor_ref[...] = first_factor
     inverse_ref[...] = first_inverse
@@ -312,7 +325,7 @@
     rest, error = two_sum(high, -lead)
     rest, more = two_sum(rest, -second)
     gap = rest + ((error + more) + (low - third))
-    gap_ref[...] = contract(contract(first_inverse, gap, nn), first_inverse, nt)
+    gap_ref[...] = times_close(times_close(first_inverse, gap), first_inverse, turned=True)
 
     left, right = gathered_pair(1)
     cross_ref[:, :ORDER] = left
@@ -356,48 +369,52 @@
 def apply_kernel(
     factor_ref, inverse_ref, gap_ref, cross_ref, panel_ref, trail_ref,
     q_ref, r_ref, p_ref, u_ref,
-    q_out, u_out, whole, store_sem,
+    q_out, r_out, p_out, u_out, whole, small_sem, store_sem,
 ):
-    nn, nt, tn = ((1,), (0,)), ((1,), (1,)), ((0,), (0,))
-    gap = gap_ref[...]
+    nn, nt = ((1,), (0,)), ((1,), (1,))
+    gap, first_factor, first_inverse = gap_ref[...], factor_ref[...], inverse_ref[...]
     rows = lax.broadcasted_iota(jnp.int32, gap.shape, 0)
     cols = lax.broadcasted_iota(jnp.int32, gap.shape, 1)
     eye = jnp.where(rows == cols, 1.0, 0.0).astype(f32)
-    weight = jnp.where(rows < cols, 1.0, 0.5 * eye).astype(f32)
-    small = jnp.sum(gap * gap) < 0.01
-
-    @pl.when(small)
-    def _():
-        first_factor, first_inverse, gap = factor_ref[...], inverse_ref[...], gap_ref[...]
-        upper = weight * gap
-        close = None
-        for step in range(4):
-            upper = weight * (gap - contract(upper, upper, tn))
-            if step == 1:
-                close = upper
-        once = first_inverse - contract(close, first_inverse, tn)
-        guess = first_inverse - contract(close, once, tn)
-        left = contract(guess, first_factor, nt)
-        rough = contract(guess, cross_ref[...], nn)
-        r_ref[...] = first_factor + contract(upper, first_factor, nn)
-        rest = (eye - left) - contract(left, upper, nt)
-        turned = guess.T
-        whole[...] = turned + contract(turned, rest, nt)
-        p_ref[...] = rough + contract(rest, rough, nn)
+    weight = jnp.where(rows > cols, 1.0, 0.5 * eye).astype(f32)
+    small = jnp.sum(gap * gap) < 0.005
+
+    start = contract(first_inverse, first_factor, nt)
+    lower = weight * gap
+    close = None
+    for step in range(STEPS):
+        lower = weight * (gap - times_close(lower, lower, turned=True))
+        if step == 0:
+            close = lower
+    guess = first_inverse - times_close(close, first_inverse)
+    guess = first_inverse - times_close(close, guess)
+    left = start - times_close(close, start)
+    left = start - times_close(close, left)
+    rough = contract(guess, cross_ref[...], nn)
+    turned = guess.T
+    rest = (eye - left) - times_close(left, lower)
+    whole[...] = turned + times_close(turned, rest, turned=True)
+    p_out[...] = rough + contract(rest, rough, nn)
+    r_out[...] = first_factor + times_close(lower.T, first_factor)
 
     @pl.when(jnp.logical_not(small))
     def _():
         second_factor, second_inverse = factor(eye + gap_ref[...])
         r_factor = contract(second_factor, factor_ref[...], nn)
-        r_ref[...] = r_factor
+        r_out[...] = r_factor
         guess = contract(second_inverse, inverse_ref[...], nn)
         inverse = guess + contract(eye - contract(guess, r_factor, nt), guess, nn)
         whole[...] = inverse.T
-        p_ref[...] = contract(inverse, cross_ref[...], nn)
-
-    inverse, projection = split(whole[...]), split(p_ref[...])
+        p_out[...] = contract(inverse, cross_ref[...], nn)
+
+    inverse, projection = split(whole[...]), split(p_out[...])
     size = panel_ref.shape[0] // CHUNKS
-    stores = []
+    stores = [
+        pltpu.make_async_copy(r_out, r_ref, small_sem.at[0]),
+        pltpu.make_async_copy(p_out, p_ref, small_sem.at[1]),
+    ]
+    stores[0].start()
+    stores[1].start()
     for k in range(CHUNKS):
         part = pl.ds(k * size, size)
         q_factor = times_square(split(panel_ref[part]), inverse)
@@ -425,11 +442,14 @@
             jax.ShapeDtypeStruct((rows, TRAIL), f32),
         ],
         in_specs=[vmem] * 6,
-        out_specs=[hbm, vmem, vmem, hbm],
+        out_specs=[hbm] * 4,
         scratch_shapes=[
             pltpu.VMEM((rows, ORDER), f32),
+            pltpu.VMEM((ORDER, ORDER), f32),
+            pltpu.VMEM((ORDER, TRAIL), f32),
             pltpu.VMEM((rows, TRAIL), f32),
             pltpu.VMEM((ORDER, ORDER), f32),
+            dma((2,)),
             dma((2, CHUNKS)),
         ],
         compiler_params=pltpu.CompilerParams(vmem_limit_bytes=32 * 2**20),

time: 35.6 us -> 33.6 us (0.944)
  Pallas kernels: 34.8 us -> 32.8 us
    pallas_call x1, Pallas kernels: 4.52 us -> 2.79 us  [applied(): pl.pallas_call(apply_kernel, out_shape=[jax.ShapeDtypeStruct((rows, ORDER...]
where the time goes in v4:
time: 33.6 us; the launch traced here: 33.5 us
  Pallas kernels  32.8 us (98%)
  between operations  0.67 us (2%)
    pallas_call x1, Pallas kernels, reduced(): pl.pallas_call(functools.partial(reduce_kernel, nz, row_total), out_shape...  30 us
    pallas_call x1, Pallas kernels, applied(): pl.pallas_call(apply_kernel, out_shape=[jax.ShapeDtypeStruct((rows, ORDER...  2.79 us

profile of v4, /device:TPU:1, one launch (start us, length us, event | category | flops | bytes accessed | tf_op | source)
XLA Modules:
  0.0 33.5 jit_solution(936877806622960996)
XLA Ops:
  0.6 0.0 copy-start
  0.6 0.0 copy-start.1
  0.7 30.0 %reduce_and_factor.1 = (f32[128,128]{1,0:T(8,128)S(1)}, f32[128,128]{1,0:T(8,128)S(1)}, f32[128,128]{1,0:T(8,128)S(1)}, f32[128,256]{1,0:T(8,128)S(1)}) custom-call(f32[512,128]{1,0:T(8,128)} %panel_ref.3, f32[512,256]{1,0:T(8,128)} %trail_ref.3), custom_call_target="tpu_custom_call" | custom-call | tf_op jit(solution)/shard_map/reduce_and_factor/pallas_call | solution.py:347
  30.7 0.0 copy-done
  30.7 0.0 copy-done.1
  30.7 2.8 %apply_factor.1 = (f32[512,128]{1,0:T(8,128)}, f32[128,128]{1,0:T(8,128)}, f32[128,256]{1,0:T(8,128)}, f32[512,256]{1,0:T(8,128)}) custom-call(f32[128,128]{1,0:T(8,128)S(1)} %get-tuple-element.8.factor_ref, f32[128,128]{1,0:T(8,128)S(1)} %get-tuple-element.9.inverse_ref, f32[128,128]{1,0:T(8,128)S(1)} %get-tuple-element.10.gap_ref, ...), custom_call_target="tpu_custom_call" | custom-call | tf_op jit(solution)/shard_map/apply_factor/pallas_call | solution.py:436
Async XLA Ops:
  0.6 30.0 %copy-start = (f32[512,256]{1,0:T(8,128)S(1)}, f32[512,256]{1,0:T(8,128)}, u32[]{:S(2)}) copy-start(f32[512,256]{1,0:T(8,128)} %trail_ref.3) | copy-start | bytes 1572868
  0.6 30.0 %copy-start.1 = (f32[512,128]{1,0:T(8,128)S(1)}, f32[512,128]{1,0:T(8,128)}, u32[]{:S(2)}) copy-start(f32[512,128]{1,0:T(8,128)} %panel_ref.3) | copy-start | bytes 786436

commit v5 on v4

--- a/solution.py
+++ b/solution.py
@@ -80,10 +80,11 @@
     row = lax.broadcasted_iota(jnp.int32, (TILE, order), 0)
     uppers, inverses = [], []
     for start in range(0, order, width):
-        top, top_inverse = work[:width], inverse[:width]
+        count = min(2 * width, order - start)
+        top, top_inverse = work[:count], inverse[:count]
         column = jnp.stack(
             [
-                jnp.broadcast_to(top[:, start + k : start + k + 1], (width, order))
+                jnp.broadcast_to(top[:, start + k : start + k + 1], (count, order))
                 for k in range(width)
             ]
         )
@@ -92,33 +93,37 @@
             r = i % TILE
             pivot = column[0, r : r + 1, :]
             held = pivot if r == 0 else jnp.where(row == r, pivot, held)
+            below = jnp.where(row > r, column[0, :TILE], 0.0)
+            if column.shape[1] > TILE:
+                below = jnp.concatenate([below, column[0, TILE:]], axis=0)
+            ratio = below * (1.0 / pivot)
             if i + 1 < width:
-                below = jnp.where(row > r, column[0, :TILE], 0.0)
-                if column.shape[1] > TILE:
-                    below = jnp.concatenate([below, column[0, TILE:]], axis=0)
-                ratio = below * (1.0 / pivot)
                 column = column[1:] - ratio[None] * column[1:, r : r + 1, :]
-                top = top - ratio * top[r : r + 1, :]
-                top_inverse = top_inverse - ratio * top_inverse[r : r + 1, :]
+            top = top - ratio * top[r : r + 1, :]
+            top_inverse = top_inverse - ratio * top_inverse[r : r + 1, :]
             if r == TILE - 1:
                 done.append(top[:TILE])
                 done_inverse.append(top_inverse[:TILE])
                 pivots.append(held)
+                if top.shape[0] > TILE:
+                    top, top_inverse = top[TILE:], top_inverse[TILE:]
                 if i + 1 < width:
-                    top, top_inverse, column = top[TILE:], top_inverse[TILE:], column[:, TILE:]
+                    column = column[:, TILE:]
         scale = lax.rsqrt(jnp.concatenate(pivots, axis=0))
         upper = jnp.concatenate(done, axis=0) * scale
         lower = jnp.concatenate(done_inverse, axis=0) * scale
         uppers.append(jnp.where(sub + start <= lane, upper, 0.0))
         inverses.append(lower)
-        if start + width < order:
+        if start + count < order:
             a0, a1, a2 = split(upper)
             b0, b1, b2 = split(jnp.concatenate([upper, lower], axis=1))
             left = jnp.concatenate([a0, a0, a1, a0, a2, a1], axis=0).T
             right = jnp.concatenate([b0, b1, b0, b2, b0, b1], axis=0)
-            step = contract(left[start + width :], right, ((1,), (0,)), None)
-            work = work[width:] - step[:, :order]
-            inverse = inverse[width:] - step[:, order:]
+            step = contract(left[start + count :], right, ((1,), (0,)), None)
+            work = jnp.concatenate([top, work[count:] - step[:, :order]], axis=0)
+            inverse = jnp.concatenate([top_inverse, inverse[count:] - step[:, order:]], axis=0)
+        else:
+            work, inverse = top, top_inverse
     return jnp.concatenate(uppers, axis=0), jnp.concatenate(inverses, axis=0)
 
 

time: 33.6 us -> 32.8 us (0.976)
  Pallas kernels: 32.8 us -> 32 us
    pallas_call x1, Pallas kernels: 30 us -> 29.2 us  [reduced(): pl.pallas_call(functools.partial(reduce_kernel, nz, row_total), out_shape...]
where the time goes in v5:
time: 32.8 us; the launch traced here: 32.7 us
  Pallas kernels  32 us (98%)
  between operations  0.67 us (2%)
    pallas_call x1, Pallas kernels, reduced(): pl.pallas_call(functools.partial(reduce_kernel, nz, row_total), out_shape...  29.2 us
    pallas_call x1, Pallas kernels, applied(): pl.pallas_call(apply_kernel, out_shape=[jax.ShapeDtypeStruct((rows, ORDER...  2.79 us

profile of v5, /device:TPU:1, one launch (start us, length us, event | category | flops | bytes accessed | tf_op | source)
XLA Modules:
  0.0 32.7 jit_solution(17372952764813335456)
XLA Ops:
  0.6 0.0 copy-start
  0.6 0.0 copy-start.1
  0.7 29.2 %reduce_and_factor.1 = (f32[128,128]{1,0:T(8,128)S(1)}, f32[128,128]{1,0:T(8,128)S(1)}, f32[128,128]{1,0:T(8,128)S(1)}, f32[128,256]{1,0:T(8,128)S(1)}) custom-call(f32[512,128]{1,0:T(8,128)} %panel_ref.3, f32[512,256]{1,0:T(8,128)} %trail_ref.3), custom_call_target="tpu_custom_call" | custom-call | tf_op jit(solution)/shard_map/reduce_and_factor/pallas_call | solution.py:352
  29.9 0.0 copy-done
  29.9 0.0 copy-done.1
  29.9 2.8 %apply_factor.1 = (f32[512,128]{1,0:T(8,128)}, f32[128,128]{1,0:T(8,128)}, f32[128,256]{1,0:T(8,128)}, f32[512,256]{1,0:T(8,128)}) custom-call(f32[128,128]{1,0:T(8,128)S(1)} %get-tuple-element.8.factor_ref, f32[128,128]{1,0:T(8,128)S(1)} %get-tuple-element.9.inverse_ref, f32[128,128]{1,0:T(8,128)S(1)} %get-tuple-element.10.gap_ref, ...), custom_call_target="tpu_custom_call" | custom-call | tf_op jit(solution)/shard_map/apply_factor/pallas_call | solution.py:441
Async XLA Ops:
  0.6 29.2 %copy-start = (f32[512,256]{1,0:T(8,128)S(1)}, f32[512,256]{1,0:T(8,128)}, u32[]{:S(2)}) copy-start(f32[512,256]{1,0:T(8,128)} %trail_ref.3) | copy-start | bytes 1572868
  0.6 29.2 %copy-start.1 = (f32[512,128]{1,0:T(8,128)S(1)}, f32[512,128]{1,0:T(8,128)}, u32[]{:S(2)}) copy-start(f32[512,128]{1,0:T(8,128)} %panel_ref.3) | copy-start | bytes 786436

commit v6 on v5

--- a/solution.py
+++ b/solution.py
@@ -210,7 +210,7 @@
     load_sem, rs_send, rs_recv, z_send, z_recv, ag_send, ag_recv,
 ):
     wide, x = lax.axis_index("wide"), lax.axis_index("narrow")
-    z, y, core = wide // (NY * NC), (wide // NC) % NY, wide % NC
+    z, y, core = lax.div(wide, NY * NC), lax.rem(lax.div(wide, NC), NY), lax.rem(wide, NC)
     share = (x * NY + y) * NC + core
 
     near = []
@@ -223,15 +223,17 @@
     near = sorted(near)
 
     def neighbour(dx, dy, dc):
-        px, py, pc = (x + dx) % NX, (y + dy) % NY, (core + dc) % NC
+        px, py, pc = lax.rem(x + dx, NX), lax.rem(y + dy, NY), lax.rem(core + dc, NC)
         return (px * NY + py) * NC + pc, ((z * NY + py) * NC + pc, px)
 
     around = [neighbour(dx, dy, dc) for _, dx, dy, dc in near]
     steps = sorted(range(1, nz), key=lambda d: -min(d, nz - d))
-    along = [((((z + d) % nz) * NY + y) * NC + core, x) for d in steps]
+    along = [((lax.rem(z + d, nz) * NY + y) * NC + core, x) for d in steps]
 
     barrier = pltpu.get_barrier_semaphore()
-    for device in [device for _, device in around] + along:
+    greeted = [(hops[0], device) for hops, (_, device) in zip(near, around)]
+    greeted += [(-min(d, nz - d), device) for d, device in zip(steps, along)]
+    for _, device in sorted(greeted, key=lambda entry: entry[0]):
         pl.semaphore_signal(barrier, inc=1, device_id=device, device_id_type=MESH)
 
     load_panel = pltpu.make_async_copy(panel_ref, panel, load_sem.at[0])
@@ -248,13 +250,13 @@
     def scatter(k):
         for slot, (target, device) in enumerate(around):
             copy(
-                send.at[k, target // NC, target % NC], rs_in.at[k, slot],
+                send.at[k, lax.div(target, NC), lax.rem(target, NC)], rs_in.at[k, slot],
                 rs_send.at[k], rs_recv.at[k], device,
             )
 
     def scattered(k):
         pltpu.make_async_copy(rs_in.at[k], rs_in.at[k], rs_recv.at[k]).wait()
-        return [send[k, share // NC, share % NC]] + [rs_in[k, n] for n in range(SHARES - 1)]
+        return [send[k, lax.div(share, NC), lax.rem(share, NC)]] + [rs_in[k, n] for n in range(SHARES - 1)]
 
     def exchange(k, block):
         z_out[k] = block

time: 32.8 us -> 32.8 us (level)
  no operation moved by 1% of the time
where the time goes in v6:
time: 32.8 us; the launch traced here: 32.7 us
  Pallas kernels  32 us (98%)
  between operations  0.67 us (2%)
    pallas_call x1, Pallas kernels, reduced(): pl.pallas_call(functools.partial(reduce_kernel, nz, row_total), out_shape...  29.2 us
    pallas_call x1, Pallas kernels, applied(): pl.pallas_call(apply_kernel, out_shape=[jax.ShapeDtypeStruct((rows, ORDER...  2.79 us

profile of v6, /device:TPU:1, one launch (start us, length us, event | category | flops | bytes accessed | tf_op | source)
XLA Modules:
  0.0 32.7 jit_solution(2327684189075061484)
XLA Ops:
  0.6 0.0 copy-start
  0.6 0.0 copy-start.1
  0.7 29.2 %reduce_and_factor.1 = (f32[128,128]{1,0:T(8,128)S(1)}, f32[128,128]{1,0:T(8,128)S(1)}, f32[128,128]{1,0:T(8,128)S(1)}, f32[128,256]{1,0:T(8,128)S(1)}) custom-call(f32[512,128]{1,0:T(8,128)} %panel_ref.3, f32[512,256]{1,0:T(8,128)} %trail_ref.3), custom_call_target="tpu_custom_call" | custom-call | tf_op jit(solution)/shard_map/reduce_and_factor/pallas_call | solution.py:354
  29.9 0.0 copy-done
  29.9 0.0 copy-done.1
  29.9 2.8 %apply_factor.1 = (f32[512,128]{1,0:T(8,128)}, f32[128,128]{1,0:T(8,128)}, f32[128,256]{1,0:T(8,128)}, f32[512,256]{1,0:T(8,128)}) custom-call(f32[128,128]{1,0:T(8,128)S(1)} %get-tuple-element.8.factor_ref, f32[128,128]{1,0:T(8,128)S(1)} %get-tuple-element.9.inverse_ref, f32[128,128]{1,0:T(8,128)S(1)} %get-tuple-element.10.gap_ref, ...), custom_call_target="tpu_custom_call" | custom-call | tf_op jit(solution)/shard_map/apply_factor/pallas_call | solution.py:443
Async XLA Ops:
  0.6 29.2 %copy-start = (f32[512,256]{1,0:T(8,128)S(1)}, f32[512,256]{1,0:T(8,128)}, u32[]{:S(2)}) copy-start(f32[512,256]{1,0:T(8,128)} %trail_ref.3) | copy-start | bytes 1572868
  0.6 29.2 %copy-start.1 = (f32[512,128]{1,0:T(8,128)S(1)}, f32[512,128]{1,0:T(8,128)}, u32[]{:S(2)}) copy-start(f32[512,128]{1,0:T(8,128)} %panel_ref.3) | copy-start | bytes 786436
